TPU v7x, 128 devices: a whole 4x4x4 slice. The times are simulated.
128 devices in a mesh: grp: 8 (over y, core), tp: 16 (over z, x).
Axes of the slice: x: 4, y: 4, z: 4, core: 2. Of those that a mesh axis runs over, the one named last changes fastest.
Arguments:
- states: bfloat16 [16384, 1280], P(('grp', 'tp')), may hold values from -6 to 6
- patch_of: int32 [16384], P(('grp', 'tp')), may hold values from 0 to 47, as said below
- targets: int32 [16384], P(('grp', 'tp')), may hold values from 0 to 255
- cotangent: float32 [16384], P(('grp', 'tp')), may hold values from -6 to 6
- w_in: bfloat16 [1280, 4096], P(None, 'tp'), may hold values from -0.15625 to 0.15625
- w_gate: bfloat16 [4096, 7168], P('grp', 'tp'), may hold values from -0.09375 to 0.09375
- w_up: bfloat16 [4096, 7168], P('grp', 'tp'), may hold values from -0.09375 to 0.09375
- w_down: bfloat16 [7168, 4096], P('tp', 'grp'), may hold values from -0.0625 to 0.0625
- w_out: bfloat16 [4096, 1280], P('tp'), may hold values from -0.09375 to 0.09375
- head_gain: float32 [1280], replicated, may hold values from 0.25 to 1.75
- w_head: bfloat16 [1280, 256], replicated, may hold values from -0.5 to 0.5
Outputs:
- log_probs: float32 [16384], P(('grp', 'tp'))
- state_grads: float32 [16384, 1280], P(('grp', 'tp'))
Inputs may be any that keep to these rules, and one draw needn't show every extreme that they name: `patch_of`: within each device's block of 128 bytes the patch number is 0 at the first byte, never falls and rises by at most one from byte to byte. A device holds at most 48 patches; each aligned block of 8 devices, in the order grp then tp, holds exactly 224 patches in all, and one device of each such block holds 48.
All inputs are finite; a program needn't handle non-finite values.
Results may differ from a plain program's by a relative error of at most 0.023.
Values may be sent and summed in bfloat16 or wider, within the bound.
A program may use at most 128 MiB of HBM per device.

v0:
```python
import jax
import jax.numpy as jnp
from jax import lax
from jax.experimental import pallas as pl
from jax.experimental.pallas import tpu as pltpu
from jax.sharding import PartitionSpec as P

BF = jnp.bfloat16
F32 = jnp.float32
MESH = pl.DeviceIdType.MESH
SIDE = 4
SLOTS = 48
N_SEMS = 288


def nn(a, b):
    return lax.dot_general(a, b, (((1,), (0,)), ((), ())), preferred_element_type=F32)


def nt(a, b):
    return lax.dot_general(a, b, (((1,), (1,)), ((), ())), preferred_element_type=F32)


def wrap(v):
    return lax.rem(v, SIDE)


def kernel(
    states, patch_of, targets, cotangent, w_in, w_gate, w_up, w_down, w_out, gain, w_head,
    log_probs, state_grads,
    raw_g, raw_u, raw_d, head_w, slab_in, slab_out, pool, fold_g, fold_u, fold_d,
    part_g, part_u, part_d, edge_g, edge_u, edge_d, mid_g, mid_u, mid_d,
    act, gate_c, up_c, hid, pout, qout, g_gate, g_up, g_mix, grads,
    rs1, rs2, mid1,
    ssem, rsem, lsem,
):
    N, E = states.shape
    EH = E // 2
    FB = w_gate.shape[0]
    DT = w_in.shape[1]
    ER = EH // SIDE
    FR = FB // SIDE
    OR = DT // SIDE
    ROWS = SIDE * SLOTS

    g = lax.axis_index("grp")
    t = lax.axis_index("tp")
    y, c = g // 2, g % 2
    z, x = t // SIDE, t % SIDE

    def X(d):
        return (g, SIDE * z + wrap(x + d))

    def Z(d):
        return (g, SIDE * wrap(z + d) + x)

    def Y(d):
        return (2 * wrap(y + d) + c, t)

    partner = (2 * y + (1 - c), t)

    sends = []
    count = [0]

    def new_sem():
        count[0] += 1
        return count[0] - 1

    def remote(src, dst, device):
        i = new_sem()
        copy = pltpu.make_async_remote_copy(
            src_ref=src, dst_ref=dst, send_sem=ssem.at[i], recv_sem=rsem.at[i],
            device_id=device, device_id_type=MESH,
        )
        copy.start()
        sends.append(copy)
        return copy

    def arrive(copies):
        for copy in copies:
            copy.wait_recv()

    barrier = pltpu.get_barrier_semaphore()
    peers = [X(d) for d in (1, 2, 3)] + [Z(d) for d in (1, 2, 3)] + [Y(1), Y(3), partner]
    for peer in peers:
        pl.semaphore_signal(barrier, 1, device_id=peer, device_id_type=MESH)

    local = [
        pltpu.make_async_copy(src, dst, lsem.at[i])
        for i, (src, dst) in enumerate(
            ((w_gate, raw_g.at[c]), (w_up, raw_u.at[c]), (w_down, raw_d.at[c]), (w_head, head_w))
        )
    ]
    for copy in local:
        copy.start()

    def column(row):
        return jnp.transpose(jnp.broadcast_to(row, (N, N)))[:, :1]

    member = patch_of[...] == lax.broadcasted_iota(jnp.int32, (SLOTS, N), 0)
    member_bf = member.astype(BF)
    divisor = jnp.maximum(jnp.sum(member.astype(F32), axis=1, keepdims=True), 1.0)
    pool[z, x] = (nn(member_bf, states[...]) / divisor).astype(BF)

    pl.semaphore_wait(barrier, len(peers))

    def spread(src_of, dst_of):
        first = [new_sem() for _ in range(SIDE)]
        out = []
        for d in range(1, SIDE):
            zz = wrap(z + d)
            out.append(
                pltpu.make_async_remote_copy(
                    src_ref=src_of(zz), dst_ref=dst_of(zz), send_sem=ssem.at[first[d]],
                    recv_sem=rsem.at[first[0]], device_id=Z(d), device_id_type=MESH,
                )
            )
        return out

    spread_in = spread(
        lambda zz: w_in.at[pl.ds(pl.multiple_of(c * EH + zz * ER, 16), ER), :],
        lambda zz: slab_in.at[zz, x],
    )

    spread_out = spread(
        lambda zz: w_out.at[
            pl.ds(pl.multiple_of(zz * OR, 16), OR), pl.ds(pl.multiple_of(c * EH, 128), EH)
        ],
        lambda zz: slab_out.at[zz, x],
    )

    def spread_start(copies):
        @pl.when(z == y)
        def _():
            for copy in copies:
                copy.start()

    def spread_arrive(copies):
        @pl.when(z != y)
        def _():
            copies[0].wait_recv()

    spread_start(spread_in)

    swap = []
    for src, dst in ((w_gate, raw_g), (w_up, raw_u), (w_down, raw_d)):
        swap.append(remote(src, dst.at[c], partner))

    @pl.when(z == y)
    def _():
        slab_in[z, x] = w_in[pl.ds(pl.multiple_of(c * EH + z * ER, 16), ER), :]
        piece = w_out[pl.ds(pl.multiple_of(z * OR, 16), OR), :]
        slab_out[z, x] = jnp.where(c == 0, piece[:, :EH], piece[:, EH:])

    def gather(buf, cut):
        def slot(h, f, s, piece=None):
            at = (wrap(z + s + 4), wrap(x + f + 4)) if h == 0 else (wrap(z + f + 4), wrap(x + s + 4))
            return buf.at[at + cut(h, piece)]

        def first(h, d):
            return X(d % SIDE) if h == 0 else Z(d % SIDE)

        def second(h, d):
            return Z(d % SIDE) if h == 0 else X(d % SIDE)

        def send(ref, device):
            return remote(ref, ref, device)

        one, two, far, last = {}, {}, {}, []
        for h in range(2):
            for d in (1, -1):
                one[h, d] = send(slot(h, 0, 0), first(h, d))
        for h in range(2):
            for d in (1, -1):
                two[h, 0, d] = send(slot(h, 0, 0), second(h, d))
        yield
        for d in (1, -1):
            for h in range(2):
                one[h, d].wait_recv()
                far[h, d] = send(slot(h, -d, 0, (1 - d) // 2), first(h, d))
                for e in (1, -1):
                    two[h, -d, e] = send(slot(h, -d, 0), second(h, e))
        yield

        def onward(f):
            for d in (1, -1):
                for h in range(2):
                    two[h, f, d].wait_recv()
                    last.append(send(slot(h, f, -d, (1 - d) // 2), second(h, d)))

        onward(0)
        yield
        for h in range(2):
            far[h, 1].wait_recv()
            far[h, -1].wait_recv()
            for e in (1, -1):
                two[h, 2, e] = send(slot(h, 2, 0), second(h, e))
        yield
        onward(-1)
        onward(1)
        yield
        onward(2)
        yield
        arrive(last)

    def cut_rows(rows, split):
        def cut(h, piece):
            lo, hi = h * rows // 2, (h + 1) * rows // 2
            mid = lo + split[h]
            if piece == 0:
                hi = mid
            elif piece == 1:
                lo = mid
            return (slice(lo, hi), slice(None))
        return cut

    def cut_cols(h, piece):
        lo, hi = h * EH, (h + 1) * EH
        mid = lo + (384 if h == 0 else 256)
        if piece == 0:
            hi = mid
        elif piece == 1:
            lo = mid
        return (slice(None), slice(lo, hi))

    def run(gen):
        for _ in gen:
            pass

    in_g = gather(slab_in, cut_rows(ER, (48, 32)))
    out_g = gather(slab_out, cut_rows(OR, (16, 16)))
    pool_g = gather(pool, cut_cols)

    spread_arrive(spread_in)
    next(in_g)
    next(pool_g)
    for _ in range(4):
        next(in_g)
    spread_start(spread_out)
    run(in_g)
    arrive(swap[:2])
    for copy in local[:2]:
        copy.wait()

    def block_in(raw):
        def f(b):
            total = jnp.zeros((ER, FB), F32)
            for xx in range(SIDE):
                lo = (xx % 2) * DT
                total += nt(slab_in[b, xx], raw[xx // 2, :, lo:lo + DT])
            return total
        return f

    def block_down(b):
        rows = pl.ds(pl.multiple_of(b * FR, 16), FR)
        total = jnp.zeros((FR, EH), F32)
        for xx in range(SIDE):
            lo = (xx % 2) * DT
            total += nn(raw_d[xx // 2, rows, lo:lo + DT], slab_out[:, xx].reshape(DT, EH))
        return total

    class Fold:
        def __init__(self, block, part, edge, mid, out, split):
            self.block, self.part, self.edge, self.mid, self.out, self.split = block, part, edge, mid, out, split

        def step_1(self):
            self.part[2] = self.block(wrap(y + 2)).astype(BF)
            s = self.split
            self.one = [
                remote(self.part.at[2, :s], self.edge.at[0, :s], Y(1)),
                remote(self.part.at[2, s:], self.edge.at[1, s:], Y(3)),
            ]

        def compute(self):
            for d in (1, 3, 0):
                self.part[d] = self.block(wrap(y + d)).astype(BF)

        def step_2(self):
            s = self.split
            self.one[0].wait_recv()
            self.part[1, :s] = (self.part[1, :s].astype(F32) + self.edge[0, :s].astype(F32)).astype(BF)
            two = [remote(self.part.at[1], self.mid.at[0], Y(1))]
            self.one[1].wait_recv()
            self.part[3, s:] = (self.part[3, s:].astype(F32) + self.edge[1, s:].astype(F32)).astype(BF)
            self.two = two + [remote(self.part.at[3], self.mid.at[1], Y(3))]

        def step_3(self):
            arrive(self.two)
            total = self.part[0].astype(F32) + self.mid[0].astype(F32) + self.mid[1].astype(F32)
            self.out[c, y] = total.astype(BF)
            own = self.out.at[c, y]
            self.three = [remote(own, own, Y(1)), remote(own, own, Y(3))]
            self.cross = [remote(own, own, partner)]

        def step_4(self):
            s = self.split
            self.three[0].wait_recv()
            low = self.out.at[c, wrap(y + 3)]
            four = [remote(low.at[:s], low.at[:s], Y(1))]
            self.cross.append(remote(low, low, partner))
            self.three[1].wait_recv()
            high = self.out.at[c, wrap(y + 1)]
            four.append(remote(high.at[s:], high.at[s:], Y(3)))
            self.cross.append(remote(high, high, partner))
            self.four = four

        def step_5(self):
            arrive(self.four)
            far = self.out.at[c, wrap(y + 2)]
            self.cross.append(remote(far, far, partner))
            arrive(self.cross)

    gate_f = Fold(block_in(raw_g), part_g, edge_g, mid_g, fold_g, ER // 2)
    up_f = Fold(block_in(raw_u), part_u, edge_u, mid_u, fold_u, ER // 2)
    down_f = Fold(block_down, part_d, edge_d, mid_d, fold_d, 64)

    gate_f.step_1()
    up_f.step_1()
    next(pool_g)
    gate_f.compute()
    up_f.compute()
    gate_f.step_2()
    spread_arrive(spread_out)
    next(out_g)
    up_f.step_2()
    next(pool_g)
    next(out_g)
    gate_f.step_3()
    next(out_g)
    next(pool_g)
    up_f.step_3()
    next(out_g)
    next(pool_g)
    gate_f.step_4()
    next(out_g)
    next(out_g)
    next(pool_g)
    up_f.step_4()
    run(out_g)
    arrive(swap[2:])
    local[2].wait()
    down_f.step_1()
    down_f.compute()
    run(pool_g)
    gate_f.step_5()
    up_f.step_5()

    def forward(i, carry):
        rows = pool[i].reshape(ROWS, E)
        act[i] = nn(rows, w_in[...]).astype(BF)
        gate_pre = nn(rows, fold_g[...].reshape(E, FB))
        up_pre = nn(rows, fold_u[...].reshape(E, FB))
        s = 1.0 / (1.0 + jnp.exp(-gate_pre))
        silu = gate_pre * s
        hid[i] = (silu * up_pre).astype(BF)
        gate_c[i] = up_pre * s * (1.0 + gate_pre * (1.0 - s))
        up_c[i] = silu
        return carry

    lax.fori_loop(0, 2, forward, 0)
    down_f.step_2()
    lax.fori_loop(2, SIDE, forward, 0)
    down_f.step_3()
    down_f.step_4()
    down_f.step_5()

    def scatter_sum(k, fill, buf):
        one, two = {}, {}

        def cols(h):
            return slice(h * EH, (h + 1) * EH)

        def send_one(h, q):
            for p in (1, 3, 2):
                at = (wrap(z + p), wrap(x + q)) if h == 0 else (wrap(z + q), wrap(x + p))
                one[h, q, p] = remote(
                    buf.at[at + (slice(None), cols(h))], rs1.at[k, h, p - 1, q], Z(p) if h == 0 else X(p)
                )

        fill(wrap(z + 2), 1)
        send_one(1, 2)
        for d in (1, 3, 2):
            fill(wrap(z + d), 0)
        for q in (2, 1, 3, 0):
            send_one(0, q)
        for q in (1, 3, 0):
            fill(wrap(z + q), 1)
            send_one(1, q)
        fill(z, 0)
        halves = {}
        for q in (2, 1, 3, 0):
            for h in (1, 0):
                at = (z, wrap(x + q)) if h == 0 else (wrap(z + q), x)
                for p in (1, 3, 2):
                    one[h, q, p].wait_recv()
                total = buf[at + (slice(None), cols(h))].astype(F32)
                for p in range(SIDE - 1):
                    total += rs1[k, h, p, q].astype(F32)
                if q:
                    mid1[k, h, q] = total.astype(BF)
                    two[h, q] = remote(
                        mid1.at[k, h, q], rs2.at[k, h, q - 1], X(q) if h == 0 else Z(q)
                    )
                else:
                    halves[h] = total
        for h in range(2):
            total = halves[h]
            for q in (1, 3, 2):
                two[h, q].wait_recv()
                total += rs2[k, h, q - 1].astype(F32)
            halves[h] = total.astype(BF)
        return jnp.concatenate([halves[0], halves[1]], axis=1)

    def fill_out(i, h):
        term = nn(hid[i], fold_d[h].reshape(FB, EH)) + nn(act[i], w_out[:, h * EH:(h + 1) * EH])
        pout[i, :, :, h * EH:(h + 1) * EH] = term.astype(BF).reshape(SIDE, SLOTS, EH)

    patch_out = scatter_sum(0, fill_out, pout)

    patch_col = column(patch_of[...])
    member_t = patch_col == lax.broadcasted_iota(jnp.int32, (N, SLOTS), 1)
    member_t_bf = member_t.astype(BF)
    decoder_in = states[...].astype(F32) + nn(member_t_bf, patch_out)
    inverse = lax.rsqrt(jnp.mean(decoder_in * decoder_in, axis=1, keepdims=True) + 1e-06)
    normal_part = decoder_in * inverse
    gains = gain[...].reshape(1, E)
    normed = (normal_part * gains).astype(BF)
    local[3].wait()
    logits = nn(normed, head_w[...])
    log_total = jnp.log(jnp.sum(jnp.exp(logits), axis=1, keepdims=True))
    is_target = column(targets[...]) == lax.broadcasted_iota(jnp.int32, logits.shape, 1)
    chosen = jnp.sum(jnp.where(is_target, logits, 0.0), axis=1, keepdims=True)
    log_probs[...] = jnp.transpose(jnp.broadcast_to(chosen - log_total, (N, N)))[:1, :]
    probs = jnp.exp(logits - log_total)
    logit_grads = (column(cotangent[...]) * (is_target.astype(F32) - probs)).astype(BF)
    scaled = nt(logit_grads, head_w[...]) * gains
    decoder_grads = inverse * (
        scaled - normal_part * jnp.mean(scaled * normal_part, axis=1, keepdims=True)
    )
    high = decoder_grads.astype(BF)
    low = (decoder_grads - high.astype(F32)).astype(BF)
    grads[z, x] = (nn(member_bf, high) + nn(member_bf, low)).astype(BF)

    grads_g = gather(grads, cut_cols)
    next(grads_g)
    state_grads[...] = decoder_grads
    run(grads_g)

    def backward(i, carry):
        rows = grads[i].reshape(ROWS, E)
        hidden_grads = nt(rows[:, :EH], fold_d[0].reshape(FB, EH)) + nt(rows[:, EH:], fold_d[1].reshape(FB, EH))
        g_gate[i] = (hidden_grads * gate_c[i]).astype(BF)
        g_up[i] = (hidden_grads * up_c[i]).astype(BF)
        g_mix[i] = nt(rows, w_out[...]).astype(BF)
        return carry

    lax.fori_loop(0, SIDE, backward, 0)

    def fill_grads(i, h):
        term = (
            nt(g_gate[i], fold_g[h].reshape(EH, FB))
            + nt(g_up[i], fold_u[h].reshape(EH, FB))
            + nt(g_mix[i], w_in[h * EH:(h + 1) * EH, :])
        )
        qout[i, :, :, h * EH:(h + 1) * EH] = term.astype(BF).reshape(SIDE, SLOTS, EH)

    pooled_grads = scatter_sum(1, fill_grads, qout)
    divisor_row = jnp.maximum(jnp.sum(member_t.astype(F32), axis=0, keepdims=True), 1.0)
    byte_divisor = jnp.sum(jnp.where(member_t, divisor_row, 0.0), axis=1, keepdims=True)
    state_grads[...] += nn(member_t_bf, pooled_grads) / byte_divisor

    @pl.when(z == y)
    def _():
        for copy in spread_in + spread_out:
            copy.wait_send()

    for copy in sends:
        copy.wait_send()


def body(
    states, patch_of, targets, cotangent, w_in, w_gate, w_up, w_down, w_out, head_gain, w_head
):
    n, E = states.shape
    DT = w_in.shape[1]
    DG, FB = w_gate.shape
    V = w_head.shape[1]
    EH = E // 2
    ER, FR, OR = EH // SIDE, FB // SIDE, DT // SIDE
    ROWS = SIDE * SLOTS
    vmem = lambda *shape: pltpu.VMEM(shape, BF)
    vmem32 = lambda *shape: pltpu.VMEM(shape, F32)
    scratch = [
        vmem(2, FB, DG), vmem(2, FB, DG), vmem(2, FB, DG), vmem(E, V),
        vmem(SIDE, SIDE, ER, DT), vmem(SIDE, SIDE, OR, EH),
        vmem(SIDE, SIDE, SLOTS, E),
        vmem(2, SIDE, ER, FB), vmem(2, SIDE, ER, FB), vmem(2, SIDE, FR, EH),
        vmem(SIDE, ER, FB), vmem(SIDE, ER, FB), vmem(SIDE, FR, EH),
        vmem(2, ER, FB), vmem(2, ER, FB), vmem(2, FR, EH),
        vmem(2, ER, FB), vmem(2, ER, FB), vmem(2, FR, EH),
        vmem(SIDE, ROWS, DT),
        vmem32(SIDE, ROWS, FB), vmem32(SIDE, ROWS, FB),
        vmem(SIDE, ROWS, FB),
        vmem(SIDE, SIDE, SLOTS, E), vmem(SIDE, SIDE, SLOTS, E),
        vmem(SIDE, ROWS, FB), vmem(SIDE, ROWS, FB), vmem(SIDE, ROWS, DT),
        vmem(SIDE, SIDE, SLOTS, E),
        vmem(2, 2, SIDE - 1, SIDE, SLOTS, EH), vmem(2, 2, SIDE - 1, SLOTS, EH),
        vmem(2, 2, SIDE, SLOTS, EH),
        pltpu.SemaphoreType.DMA((N_SEMS,)), pltpu.SemaphoreType.DMA((N_SEMS,)),
        pltpu.SemaphoreType.DMA((4,)),
    ]
    near = pl.BlockSpec(memory_space=pltpu.VMEM)
    away = pl.BlockSpec(memory_space=pl.ANY)
    log_probs, state_grads = pl.pallas_call(
        kernel,
        out_shape=(jax.ShapeDtypeStruct((1, n), F32), jax.ShapeDtypeStruct((n, E), F32)),
        in_specs=[near] * 5 + [away] * 3 + [near] * 2 + [away],
        out_specs=(near, near),
        scratch_shapes=scratch,
        compiler_params=pltpu.CompilerParams(
            collective_id=0, has_side_effects=True, vmem_limit_bytes=60 * 2**20
        ),
        name="patch_step",
    )(
        states, patch_of.reshape(1, n), targets.reshape(1, n), cotangent.reshape(1, n),
        w_in, w_gate.T, w_up.T, w_down, w_out, head_gain, w_head,
    )
    return log_probs.reshape(n), state_grads


def solution(mesh):
    return jax.shard_map(
        body,
        mesh=mesh,
        in_specs=(
            P(("grp", "tp"), None),
            P(("grp", "tp")),
            P(("grp", "tp")),
            P(("grp", "tp")),
            P(None, "tp"),
            P("grp", "tp"),
            P("grp", "tp"),
            P("tp", "grp"),
            P("tp", None),
            P(),
            P(),
        ),
        out_specs=(P(("grp", "tp")), P(("grp", "tp"), None)),
        check_vma=False,
    )
```

profile of v0, /device:TPU:0, one launch (start us, length us, event | category | flops | bytes accessed | tf_op | source)
XLA Modules:
  0.0 136.3 jit_solution(12437592168445268530)
XLA Ops:
  0.6 132.6 %patch_step.1 = (f32[1,128]{1,0:T(1,128)}, f32[128,1280]{1,0:T(8,128)}) custom-call(bf16[128,1280]{1,0:T(8,128)(2,1)} %states.1, s32[1,128]{1,0:T(1,128)} %bitcast.8, s32[1,128]{1,0:T(1,128)} %bitcast.9, f32[1,128]{1,0:T(1,128)} %bitcast.10, bf16[1280,256]{1,0:T(8,128)(2,1)} %w_in.1, bf16[448,512]{1,0:T(8,128)(2,1)} %bitcast.6, bf16[448,512]{1,0:T(8,128)(2,1)} %bitcast.7, ...), custom_call_target="tpu_custom_call" | custom-call | tf_op jit(solution)/shard_map/patch_step/pallas_call | solution.py:514
  133.2 0.0 copy-start
  133.2 0.6 copy-done
  133.9 0.5 copy.15
  134.4 2.0 %copy.16 = f32[128,1280]{1,0:T(8,128)} copy(f32[128,1280]{1,0:T(8,128)} %get-tuple-element.9) | data formatting | bytes 1310720
Async XLA Ops:
  133.2 0.6 copy-start
where the time goes:
time: 137 us; the launch traced here: 136 us
  Pallas kernels  133 us (97%)
  local copies, waits for them, and re-layouts  3.1 us (2%)
    pallas_call x1, Pallas kernels, body(): pl.pallas_call(kernel, out_shape=(jax.ShapeDtypeStruct((1, n), F32), jax....  133 us
    unnamed x4, local copies, waits for them, and re-layouts  3.1 us

commit v1 on v0

--- a/solution.py
+++ b/solution.py
@@ -10,7 +10,7 @@
 MESH = pl.DeviceIdType.MESH
 SIDE = 4
 SLOTS = 48
-N_SEMS = 288
+N_SEMS = 256
 
 
 def nn(a, b):
@@ -141,6 +141,7 @@
             copies[0].wait_recv()
 
     spread_start(spread_in)
+    spread_start(spread_out)
 
     swap = []
     for src, dst in ((w_gate, raw_g), (w_up, raw_u), (w_down, raw_d)):
@@ -152,56 +153,45 @@
         piece = w_out[pl.ds(pl.multiple_of(z * OR, 16), OR), :]
         slab_out[z, x] = jnp.where(c == 0, piece[:, :EH], piece[:, EH:])
 
-    def gather(buf, cut):
+    def gather(buf, cut, ring):
         def slot(h, f, s, piece=None):
             at = (wrap(z + s + 4), wrap(x + f + 4)) if h == 0 else (wrap(z + f + 4), wrap(x + s + 4))
             return buf.at[at + cut(h, piece)]
 
         def first(h, d):
-            return X(d % SIDE) if h == 0 else Z(d % SIDE)
+            return X(d) if h == 0 else Z(d)
 
         def second(h, d):
-            return Z(d % SIDE) if h == 0 else X(d % SIDE)
+            return Z(d) if h == 0 else X(d)
 
         def send(ref, device):
             return remote(ref, ref, device)
 
-        one, two, far, last = {}, {}, {}, []
-        for h in range(2):
-            for d in (1, -1):
+        ways = (1, 3) if ring else (1, 3, 2)
+        one, two, last = {}, {}, []
+        for d in (1, 3, 2):
+            for h in range(2):
                 one[h, d] = send(slot(h, 0, 0), first(h, d))
-        for h in range(2):
-            for d in (1, -1):
-                two[h, 0, d] = send(slot(h, 0, 0), second(h, d))
+        for e in ways:
+            for h in range(2):
+                two[h, 0, e] = send(slot(h, 0, 0), second(h, e))
         yield
-        for d in (1, -1):
+        for d in (1, 3, 2):
             for h in range(2):
                 one[h, d].wait_recv()
-                far[h, d] = send(slot(h, -d, 0, (1 - d) // 2), first(h, d))
-                for e in (1, -1):
-                    two[h, -d, e] = send(slot(h, -d, 0), second(h, e))
+                for e in ways:
+                    two[h, d, e] = send(slot(h, -d, 0), second(h, e))
         yield
-
-        def onward(f):
-            for d in (1, -1):
-                for h in range(2):
-                    two[h, f, d].wait_recv()
-                    last.append(send(slot(h, f, -d, (1 - d) // 2), second(h, d)))
-
-        onward(0)
-        yield
-        for h in range(2):
-            far[h, 1].wait_recv()
-            far[h, -1].wait_recv()
-            for e in (1, -1):
-                two[h, 2, e] = send(slot(h, 2, 0), second(h, e))
-        yield
-        onward(-1)
-        onward(1)
-        yield
-        onward(2)
-        yield
-        arrive(last)
+        if ring:
+            for d in (0, 1, 3, 2):
+                for e in ways:
+                    for h in range(2):
+                        two[h, d, e].wait_recv()
+                        last.append(send(slot(h, -d, -e, e // 2), second(h, e)))
+                yield
+            arrive(last)
+        else:
+            arrive(two.values())
 
     def cut_rows(rows, split):
         def cut(h, piece):
@@ -227,66 +217,62 @@
         for _ in gen:
             pass
 
-    in_g = gather(slab_in, cut_rows(ER, (48, 32)))
-    out_g = gather(slab_out, cut_rows(OR, (16, 16)))
-    pool_g = gather(pool, cut_cols)
+    in_g = gather(slab_in, cut_rows(ER, (48, 32)), False)
+    out_g = gather(slab_out, cut_rows(OR, (16, 16)), False)
+    pool_g = gather(pool, cut_cols, True)
 
     spread_arrive(spread_in)
     next(in_g)
-    next(pool_g)
-    for _ in range(4):
-        next(in_g)
-    spread_start(spread_out)
+    next(in_g)
+    spread_arrive(spread_out)
+    next(out_g)
     run(in_g)
     arrive(swap[:2])
     for copy in local[:2]:
         copy.wait()
 
     def block_in(raw):
-        def f(b):
-            total = jnp.zeros((ER, FB), F32)
+        def f():
+            total = jnp.zeros((EH, FB), F32)
             for xx in range(SIDE):
                 lo = (xx % 2) * DT
-                total += nt(slab_in[b, xx], raw[xx // 2, :, lo:lo + DT])
-            return total
+                total += nt(slab_in[:, xx].reshape(EH, DT), raw[xx // 2, :, lo:lo + DT])
+            return total.astype(BF).reshape(SIDE, ER, FB)
         return f
 
-    def block_down(b):
-        rows = pl.ds(pl.multiple_of(b * FR, 16), FR)
-        total = jnp.zeros((FR, EH), F32)
+    def block_down():
+        total = jnp.zeros((FB, EH), F32)
         for xx in range(SIDE):
             lo = (xx % 2) * DT
-            total += nn(raw_d[xx // 2, rows, lo:lo + DT], slab_out[:, xx].reshape(DT, EH))
-        return total
+            total += nn(raw_d[xx // 2, :, lo:lo + DT], slab_out[:, xx].reshape(DT, EH))
+        return total.astype(BF).reshape(SIDE, FR, EH)
 
     class Fold:
         def __init__(self, block, part, edge, mid, out, split):
             self.block, self.part, self.edge, self.mid, self.out, self.split = block, part, edge, mid, out, split
 
         def step_1(self):
-            self.part[2] = self.block(wrap(y + 2)).astype(BF)
+            self.part[...] = self.block()
             s = self.split
+            far = wrap(y + 2)
             self.one = [
-                remote(self.part.at[2, :s], self.edge.at[0, :s], Y(1)),
-                remote(self.part.at[2, s:], self.edge.at[1, s:], Y(3)),
+                remote(self.part.at[far, :s], self.edge.at[0, :s], Y(1)),
+                remote(self.part.at[far, s:], self.edge.at[1, s:], Y(3)),
             ]
-
-        def compute(self):
-            for d in (1, 3, 0):
-                self.part[d] = self.block(wrap(y + d)).astype(BF)
 
         def step_2(self):
             s = self.split
+            right, left = wrap(y + 1), wrap(y + 3)
             self.one[0].wait_recv()
-            self.part[1, :s] = (self.part[1, :s].astype(F32) + self.edge[0, :s].astype(F32)).astype(BF)
-            two = [remote(self.part.at[1], self.mid.at[0], Y(1))]
+            self.part[right, :s] = (self.part[right, :s].astype(F32) + self.edge[0, :s].astype(F32)).astype(BF)
+            two = [remote(self.part.at[right], self.mid.at[0], Y(1))]
             self.one[1].wait_recv()
-            self.part[3, s:] = (self.part[3, s:].astype(F32) + self.edge[1, s:].astype(F32)).astype(BF)
-            self.two = two + [remote(self.part.at[3], self.mid.at[1], Y(3))]
+            self.part[left, s:] = (self.part[left, s:].astype(F32) + self.edge[1, s:].astype(F32)).astype(BF)
+            self.two = two + [remote(self.part.at[left], self.mid.at[1], Y(3))]
 
         def step_3(self):
             arrive(self.two)
-            total = self.part[0].astype(F32) + self.mid[0].astype(F32) + self.mid[1].astype(F32)
+            total = self.part[y].astype(F32) + self.mid[0].astype(F32) + self.mid[1].astype(F32)
             self.out[c, y] = total.astype(BF)
             own = self.out.at[c, y]
             self.three = [remote(own, own, Y(1)), remote(own, own, Y(3))]
@@ -316,34 +302,27 @@
 
     gate_f.step_1()
     up_f.step_1()
-    next(pool_g)
-    gate_f.compute()
-    up_f.compute()
-    gate_f.step_2()
-    spread_arrive(spread_out)
-    next(out_g)
-    up_f.step_2()
-    next(pool_g)
-    next(out_g)
-    gate_f.step_3()
     next(out_g)
     next(pool_g)
-    up_f.step_3()
-    next(out_g)
-    next(pool_g)
-    gate_f.step_4()
-    next(out_g)
-    next(out_g)
-    next(pool_g)
-    up_f.step_4()
+    gate_f.step_2()
+    up_f.step_2()
     run(out_g)
     arrive(swap[2:])
     local[2].wait()
     down_f.step_1()
-    down_f.compute()
-    run(pool_g)
+    next(pool_g)
+    gate_f.step_3()
+    up_f.step_3()
+    down_f.step_2()
+    next(pool_g)
+    gate_f.step_4()
+    up_f.step_4()
+    next(pool_g)
+    down_f.step_3()
+    next(pool_g)
     gate_f.step_5()
     up_f.step_5()
+    run(pool_g)
 
     def forward(i, carry):
         rows = pool[i].reshape(ROWS, E)
@@ -358,10 +337,8 @@
         return carry
 
     lax.fori_loop(0, 2, forward, 0)
-    down_f.step_2()
+    down_f.step_4()
     lax.fori_loop(2, SIDE, forward, 0)
-    down_f.step_3()
-    down_f.step_4()
     down_f.step_5()
 
     def scatter_sum(k, fill, buf):
@@ -370,23 +347,20 @@
         def cols(h):
             return slice(h * EH, (h + 1) * EH)
 
-        def send_one(h, q):
+        def send_one(h, p, q):
+            at = (wrap(z + p), wrap(x + q)) if h == 0 else (wrap(z + q), wrap(x + p))
+            one[h, q, p] = remote(
+                buf.at[at + (slice(None), cols(h))], rs1.at[k, h, p - 1, q], Z(p) if h == 0 else X(p)
+            )
+
+        for d in (2, 1, 3, 0):
+            fill(wrap(z + d), 0)
+            if d:
+                for q in (2, 1, 3, 0):
+                    send_one(0, d, q)
+            fill(wrap(z + d), 1)
             for p in (1, 3, 2):
-                at = (wrap(z + p), wrap(x + q)) if h == 0 else (wrap(z + q), wrap(x + p))
-                one[h, q, p] = remote(
-                    buf.at[at + (slice(None), cols(h))], rs1.at[k, h, p - 1, q], Z(p) if h == 0 else X(p)
-                )
-
-        fill(wrap(z + 2), 1)
-        send_one(1, 2)
-        for d in (1, 3, 2):
-            fill(wrap(z + d), 0)
-        for q in (2, 1, 3, 0):
-            send_one(0, q)
-        for q in (1, 3, 0):
-            fill(wrap(z + q), 1)
-            send_one(1, q)
-        fill(z, 0)
+                send_one(1, p, d)
         halves = {}
         for q in (2, 1, 3, 0):
             for h in (1, 0):
@@ -441,7 +415,7 @@
     low = (decoder_grads - high.astype(F32)).astype(BF)
     grads[z, x] = (nn(member_bf, high) + nn(member_bf, low)).astype(BF)
 
-    grads_g = gather(grads, cut_cols)
+    grads_g = gather(grads, cut_cols, True)
     next(grads_g)
     state_grads[...] = decoder_grads
     run(grads_g)

time: 137 us -> 129 us (0.942)
  Pallas kernels: 133 us -> 125 us
    pallas_call x1, Pallas kernels: 133 us -> 125 us  [body(): pl.pallas_call(kernel, out_shape=(jax.ShapeDtypeStruct((1, n), F32), jax....]
where the time goes in v1:
time: 129 us
  Pallas kernels  125 us (97%)
  local copies, waits for them, and re-layouts  3.1 us (2%)
    pallas_call x1, Pallas kernels, body(): pl.pallas_call(kernel, out_shape=(jax.ShapeDtypeStruct((1, n), F32), jax....  125 us
    unnamed x4, local copies, waits for them, and re-layouts  3.1 us

profile of v1, /device:TPU:0, one launch (start us, length us, event | category | flops | bytes accessed | tf_op | source)
XLA Modules:
  0.0 128.9 jit_solution(11080540907139503356)
XLA Ops:
  0.6 125.2 %patch_step.1 = (f32[1,128]{1,0:T(1,128)}, f32[128,1280]{1,0:T(8,128)}) custom-call(bf16[128,1280]{1,0:T(8,128)(2,1)} %states.1, s32[1,128]{1,0:T(1,128)} %bitcast.8, s32[1,128]{1,0:T(1,128)} %bitcast.9, f32[1,128]{1,0:T(1,128)} %bitcast.10, bf16[1280,256]{1,0:T(8,128)(2,1)} %w_in.1, bf16[448,512]{1,0:T(8,128)(2,1)} %bitcast.6, bf16[448,512]{1,0:T(8,128)(2,1)} %bitcast.7, ...), custom_call_target="tpu_custom_call" | custom-call | tf_op jit(solution)/shard_map/patch_step/pallas_call | solution.py:488
  125.8 0.0 copy-start
  125.8 0.6 copy-done
  126.5 0.5 copy.15
  127.0 2.0 %copy.16 = f32[128,1280]{1,0:T(8,128)} copy(f32[128,1280]{1,0:T(8,128)} %get-tuple-element.9) | data formatting | bytes 1310720
Async XLA Ops:
  125.8 0.6 copy-start

commit v2 on v1

--- a/solution.py
+++ b/solution.py
@@ -219,7 +219,7 @@
 
     in_g = gather(slab_in, cut_rows(ER, (48, 32)), False)
     out_g = gather(slab_out, cut_rows(OR, (16, 16)), False)
-    pool_g = gather(pool, cut_cols, True)
+    pool_g = gather(pool, cut_cols, False)
 
     spread_arrive(spread_in)
     next(in_g)
@@ -249,10 +249,12 @@
 
     class Fold:
         def __init__(self, block, part, edge, mid, out, split):
-            self.block, self.part, self.edge, self.mid, self.out, self.split = block, part, edge, mid, out, split
+            self.block, self.part, self.edge, self.mid, self.split = block, part, edge, mid, split
+            self.out = out
 
         def step_1(self):
-            self.part[...] = self.block()
+            if self.block is not None:
+                self.part[...] = self.block()
             s = self.split
             far = wrap(y + 2)
             self.one = [
@@ -273,32 +275,43 @@
         def step_3(self):
             arrive(self.two)
             total = self.part[y].astype(F32) + self.mid[0].astype(F32) + self.mid[1].astype(F32)
-            self.out[c, y] = total.astype(BF)
-            own = self.out.at[c, y]
+            own = self.out(y)
+            own[...] = total.astype(BF)
             self.three = [remote(own, own, Y(1)), remote(own, own, Y(3))]
             self.cross = [remote(own, own, partner)]
 
         def step_4(self):
             s = self.split
             self.three[0].wait_recv()
-            low = self.out.at[c, wrap(y + 3)]
+            low = self.out(wrap(y + 3))
             four = [remote(low.at[:s], low.at[:s], Y(1))]
             self.cross.append(remote(low, low, partner))
             self.three[1].wait_recv()
-            high = self.out.at[c, wrap(y + 1)]
+            high = self.out(wrap(y + 1))
             four.append(remote(high.at[s:], high.at[s:], Y(3)))
             self.cross.append(remote(high, high, partner))
             self.four = four
 
         def step_5(self):
             arrive(self.four)
-            far = self.out.at[c, wrap(y + 2)]
+            far = self.out(wrap(y + 2))
             self.cross.append(remote(far, far, partner))
             arrive(self.cross)
 
-    gate_f = Fold(block_in(raw_g), part_g, edge_g, mid_g, fold_g, ER // 2)
-    up_f = Fold(block_in(raw_u), part_u, edge_u, mid_u, fold_u, ER // 2)
-    down_f = Fold(block_down, part_d, edge_d, mid_d, fold_d, 64)
+    gate_f = Fold(block_in(raw_g), part_g, edge_g, mid_g, lambda yy: fold_g.at[c, yy], ER // 2)
+    up_f = Fold(block_in(raw_u), part_u, edge_u, mid_u, lambda yy: fold_u.at[c, yy], ER // 2)
+
+    def fold_down(rows, split):
+        return Fold(
+            None, part_d.at[:, rows], edge_d.at[:, rows], mid_d.at[:, rows],
+            lambda yy: fold_d.at[c, yy, rows], split,
+        )
+
+    downs = [fold_down(slice(0, 64), 32), fold_down(slice(64, FR), 32)]
+
+    def down_step(name):
+        for fold in downs:
+            getattr(fold, name)()
 
     gate_f.step_1()
     up_f.step_1()
@@ -309,17 +322,15 @@
     run(out_g)
     arrive(swap[2:])
     local[2].wait()
-    down_f.step_1()
+    part_d[...] = block_down()
+    down_step("step_1")
     next(pool_g)
     gate_f.step_3()
     up_f.step_3()
-    down_f.step_2()
-    next(pool_g)
+    down_step("step_2")
     gate_f.step_4()
     up_f.step_4()
-    next(pool_g)
-    down_f.step_3()
-    next(pool_g)
+    down_step("step_3")
     gate_f.step_5()
     up_f.step_5()
     run(pool_g)
@@ -336,10 +347,10 @@
         up_c[i] = silu
         return carry
 
-    lax.fori_loop(0, 2, forward, 0)
-    down_f.step_4()
-    lax.fori_loop(2, SIDE, forward, 0)
-    down_f.step_5()
+    lax.fori_loop(0, 1, forward, 0)
+    down_step("step_4")
+    lax.fori_loop(1, SIDE, forward, 0)
+    down_step("step_5")
 
     def scatter_sum(k, fill, buf):
         one, two = {}, {}
@@ -353,14 +364,27 @@
                 buf.at[at + (slice(None), cols(h))], rs1.at[k, h, p - 1, q], Z(p) if h == 0 else X(p)
             )
 
-        for d in (2, 1, 3, 0):
+        def send_all(h, q):
+            for p in (1, 3, 2):
+                send_one(h, p, q)
+
+        fill(wrap(z + 2), 0)
+        send_one(0, 2, 2)
+        fill(wrap(z + 2), 1)
+        send_all(1, 2)
+        for d in (1, 3):
             fill(wrap(z + d), 0)
-            if d:
-                for q in (2, 1, 3, 0):
-                    send_one(0, d, q)
-            fill(wrap(z + d), 1)
-            for p in (1, 3, 2):
-                send_one(1, p, d)
+            send_one(0, d, 2)
+        send_all(0, 1)
+        fill(wrap(z + 1), 1)
+        send_all(1, 1)
+        send_all(0, 3)
+        fill(wrap(z + 3), 1)
+        send_all(1, 3)
+        send_all(0, 0)
+        fill(z, 1)
+        send_all(1, 0)
+        fill(z, 0)
         halves = {}
         for q in (2, 1, 3, 0):
             for h in (1, 0):
@@ -450,6 +474,7 @@
 
     for copy in sends:
         copy.wait_send()
+    assert count[0] <= N_SEMS
 
 
 def body(

time: 129 us -> 126 us (0.977)
  Pallas kernels: 125 us -> 122 us
    pallas_call x1, Pallas kernels: 125 us -> 122 us  [body(): pl.pallas_call(kernel, out_shape=(jax.ShapeDtypeStruct((1, n), F32), jax....]
where the time goes in v2:
time: 126 us; the launch traced here: 125 us
  Pallas kernels  122 us (97%)
  local copies, waits for them, and re-layouts  3.1 us (2%)
    pallas_call x1, Pallas kernels, body(): pl.pallas_call(kernel, out_shape=(jax.ShapeDtypeStruct((1, n), F32), jax....  122 us
    unnamed x4, local copies, waits for them, and re-layouts  3.1 us

profile of v2, /device:TPU:0, one launch (start us, length us, event | category | flops | bytes accessed | tf_op | source)
XLA Modules:
  0.0 125.5 jit_solution(6580584921759165013)
XLA Ops:
  0.6 121.7 %patch_step.1 = (f32[1,128]{1,0:T(1,128)}, f32[128,1280]{1,0:T(8,128)}) custom-call(bf16[128,1280]{1,0:T(8,128)(2,1)} %states.1, s32[1,128]{1,0:T(1,128)} %bitcast.8, s32[1,128]{1,0:T(1,128)} %bitcast.9, f32[1,128]{1,0:T(1,128)} %bitcast.10, bf16[1280,256]{1,0:T(8,128)(2,1)} %w_in.1, bf16[448,512]{1,0:T(8,128)(2,1)} %bitcast.6, bf16[448,512]{1,0:T(8,128)(2,1)} %bitcast.7, ...), custom_call_target="tpu_custom_call" | custom-call | tf_op jit(solution)/shard_map/patch_step/pallas_call | solution.py:513
  122.4 0.0 copy-start
  122.4 0.6 copy-done
  123.0 0.5 copy.15
  123.5 2.0 %copy.16 = f32[128,1280]{1,0:T(8,128)} copy(f32[128,1280]{1,0:T(8,128)} %get-tuple-element.9) | data formatting | bytes 1310720
Async XLA Ops:
  122.4 0.6 copy-start

commit v3 on v2

--- a/solution.py
+++ b/solution.py
@@ -27,7 +27,7 @@
 
 def kernel(
     states, patch_of, targets, cotangent, w_in, w_gate, w_up, w_down, w_out, gain, w_head,
-    log_probs, state_grads,
+    log_probs, state_grads, spread_grads,
     raw_g, raw_u, raw_d, head_w, slab_in, slab_out, pool, fold_g, fold_u, fold_d,
     part_g, part_u, part_d, edge_g, edge_u, edge_d, mid_g, mid_u, mid_d,
     act, gate_c, up_c, hid, pout, qout, g_gate, g_up, g_mix, grads,
@@ -319,6 +319,15 @@
     next(pool_g)
     gate_f.step_2()
     up_f.step_2()
+
+    patch_col = column(patch_of[...])
+    member_t = patch_col == lax.broadcasted_iota(jnp.int32, (N, SLOTS), 1)
+    member_t_bf = member_t.astype(BF)
+    divisor_row = jnp.maximum(jnp.sum(member_t.astype(F32), axis=0, keepdims=True), 1.0)
+    byte_divisor = jnp.sum(jnp.where(member_t, divisor_row, 0.0), axis=1, keepdims=True)
+    target_col = column(targets[...])
+    weight_col = column(cotangent[...])
+
     run(out_g)
     arrive(swap[2:])
     local[2].wait()
@@ -347,12 +356,11 @@
         up_c[i] = silu
         return carry
 
-    lax.fori_loop(0, 1, forward, 0)
     down_step("step_4")
-    lax.fori_loop(1, SIDE, forward, 0)
+    lax.fori_loop(0, SIDE, forward, 0)
     down_step("step_5")
 
-    def scatter_sum(k, fill, buf):
+    def scatter_sum(k, prepare, fill, buf):
         one, two = {}, {}
 
         def cols(h):
@@ -368,11 +376,13 @@
             for p in (1, 3, 2):
                 send_one(h, p, q)
 
+        prepare(wrap(z + 2))
         fill(wrap(z + 2), 0)
         send_one(0, 2, 2)
         fill(wrap(z + 2), 1)
         send_all(1, 2)
         for d in (1, 3):
+            prepare(wrap(z + d))
             fill(wrap(z + d), 0)
             send_one(0, d, 2)
         send_all(0, 1)
@@ -382,6 +392,7 @@
         fill(wrap(z + 3), 1)
         send_all(1, 3)
         send_all(0, 0)
+        prepare(z)
         fill(z, 1)
         send_all(1, 0)
         fill(z, 0)
@@ -413,11 +424,8 @@
         term = nn(hid[i], fold_d[h].reshape(FB, EH)) + nn(act[i], w_out[:, h * EH:(h + 1) * EH])
         pout[i, :, :, h * EH:(h + 1) * EH] = term.astype(BF).reshape(SIDE, SLOTS, EH)
 
-    patch_out = scatter_sum(0, fill_out, pout)
-
-    patch_col = column(patch_of[...])
-    member_t = patch_col == lax.broadcasted_iota(jnp.int32, (N, SLOTS), 1)
-    member_t_bf = member_t.astype(BF)
+    patch_out = scatter_sum(0, lambda i: None, fill_out, pout)
+
     decoder_in = states[...].astype(F32) + nn(member_t_bf, patch_out)
     inverse = lax.rsqrt(jnp.mean(decoder_in * decoder_in, axis=1, keepdims=True) + 1e-06)
     normal_part = decoder_in * inverse
@@ -426,11 +434,11 @@
     local[3].wait()
     logits = nn(normed, head_w[...])
     log_total = jnp.log(jnp.sum(jnp.exp(logits), axis=1, keepdims=True))
-    is_target = column(targets[...]) == lax.broadcasted_iota(jnp.int32, logits.shape, 1)
+    is_target = target_col == lax.broadcasted_iota(jnp.int32, logits.shape, 1)
     chosen = jnp.sum(jnp.where(is_target, logits, 0.0), axis=1, keepdims=True)
     log_probs[...] = jnp.transpose(jnp.broadcast_to(chosen - log_total, (N, N)))[:1, :]
     probs = jnp.exp(logits - log_total)
-    logit_grads = (column(cotangent[...]) * (is_target.astype(F32) - probs)).astype(BF)
+    logit_grads = (weight_col * (is_target.astype(F32) - probs)).astype(BF)
     scaled = nt(logit_grads, head_w[...]) * gains
     decoder_grads = inverse * (
         scaled - normal_part * jnp.mean(scaled * normal_part, axis=1, keepdims=True)
@@ -442,17 +450,25 @@
     grads_g = gather(grads, cut_cols, True)
     next(grads_g)
     state_grads[...] = decoder_grads
+
+    def sent(copies):
+        for copy in copies:
+            copy.wait_send()
+
+    @pl.when(z == y)
+    def _():
+        sent(spread_in + spread_out)
+
+    early = len(sends) - 20
+    sent(sends[:early])
     run(grads_g)
 
-    def backward(i, carry):
+    def backward(i):
         rows = grads[i].reshape(ROWS, E)
         hidden_grads = nt(rows[:, :EH], fold_d[0].reshape(FB, EH)) + nt(rows[:, EH:], fold_d[1].reshape(FB, EH))
         g_gate[i] = (hidden_grads * gate_c[i]).astype(BF)
         g_up[i] = (hidden_grads * up_c[i]).astype(BF)
         g_mix[i] = nt(rows, w_out[...]).astype(BF)
-        return carry
-
-    lax.fori_loop(0, SIDE, backward, 0)
 
     def fill_grads(i, h):
         term = (
@@ -462,18 +478,10 @@
         )
         qout[i, :, :, h * EH:(h + 1) * EH] = term.astype(BF).reshape(SIDE, SLOTS, EH)
 
-    pooled_grads = scatter_sum(1, fill_grads, qout)
-    divisor_row = jnp.maximum(jnp.sum(member_t.astype(F32), axis=0, keepdims=True), 1.0)
-    byte_divisor = jnp.sum(jnp.where(member_t, divisor_row, 0.0), axis=1, keepdims=True)
-    state_grads[...] += nn(member_t_bf, pooled_grads) / byte_divisor
-
-    @pl.when(z == y)
-    def _():
-        for copy in spread_in + spread_out:
-            copy.wait_send()
-
-    for copy in sends:
-        copy.wait_send()
+    pooled_grads = scatter_sum(1, backward, fill_grads, qout)
+    spread_grads[...] = nn(member_t_bf, pooled_grads) / byte_divisor
+
+    sent(sends[early:])
     assert count[0] <= N_SEMS
 
 
@@ -510,11 +518,11 @@
     ]
     near = pl.BlockSpec(memory_space=pltpu.VMEM)
     away = pl.BlockSpec(memory_space=pl.ANY)
-    log_probs, state_grads = pl.pallas_call(
+    log_probs, decoder_grads, spread_grads = pl.pallas_call(
         kernel,
-        out_shape=(jax.ShapeDtypeStruct((1, n), F32), jax.ShapeDtypeStruct((n, E), F32)),
+        out_shape=(jax.ShapeDtypeStruct((1, n), F32),) + (jax.ShapeDtypeStruct((n, E), F32),) * 2,
         in_specs=[near] * 5 + [away] * 3 + [near] * 2 + [away],
-        out_specs=(near, near),
+        out_specs=(near, near, near),
         scratch_shapes=scratch,
         compiler_params=pltpu.CompilerParams(
             collective_id=0, has_side_effects=True, vmem_limit_bytes=60 * 2**20
@@ -524,7 +532,7 @@
         states, patch_of.reshape(1, n), targets.reshape(1, n), cotangent.reshape(1, n),
         w_in, w_gate.T, w_up.T, w_down, w_out, head_gain, w_head,
     )
-    return log_probs.reshape(n), state_grads
+    return log_probs.reshape(n), decoder_grads + spread_grads
 
 
 def solution(mesh):

time: 126 us -> 124 us (0.984)
  local copies, waits for them, and re-layouts: 3.1 us -> 0.52 us
  other arithmetic: 0 us -> 2.19 us
    unnamed x4 -> x3, local copies, waits for them, and re-layouts: 3.1 us -> 0.52 us
    add x0 -> x1, other arithmetic: none -> 2.19 us  [body(): return (log_probs.reshape(n), decoder_grads + spread_grads)]
where the time goes in v3:
time: 124 us
  Pallas kernels  121 us (98%)
  other arithmetic  2.19 us (2%)
    pallas_call x1, Pallas kernels, body(): pl.pallas_call(kernel, out_shape=(jax.ShapeDtypeStruct((1, n), F32),) + (...  121 us

profile of v3, /device:TPU:0, one launch (start us, length us, event | category | flops | bytes accessed | tf_op | source)
XLA Modules:
  0.0 124.2 jit_solution(6039151301739119964)
XLA Ops:
  0.6 120.9 %patch_step.1 = (f32[1,128]{1,0:T(1,128)}, f32[128,1280]{1,0:T(8,128)}, f32[128,1280]{1,0:T(8,128)}) custom-call(bf16[128,1280]{1,0:T(8,128)(2,1)} %states.1, s32[1,128]{1,0:T(1,128)} %bitcast.8, s32[1,128]{1,0:T(1,128)} %bitcast.9, f32[1,128]{1,0:T(1,128)} %bitcast.10, bf16[1280,256]{1,0:T(8,128)(2,1)} %w_in.1, bf16[448,512]{1,0:T(8,128)(2,1)} %bitcast.6, ...), custom_call_target="tpu_custom_call" | custom-call | tf_op jit(solution)/shard_map/patch_step/pallas_call | solution.py:521
  121.5 0.0 copy-start
  121.5 2.2 %add.3 = f32[128,1280]{1,0:T(8,128)} add(f32[128,1280]{1,0:T(8,128)} %get-tuple-element.6, f32[128,1280]{1,0:T(8,128)} %get-tuple-element.7) | non-fusion elementwise | flops 163840 | bytes 1966080 | tf_op jit(solution)/shard_map/add | solution.py:535
  123.7 0.0 copy-done
  123.7 0.5 copy.14
Async XLA Ops:
  121.5 2.2 %copy-start = (f32[1,128]{1,0:T(1,128)S(1)}, f32[1,128]{1,0:T(1,128)}, u32[]{:S(2)}) copy-start(f32[1,128]{1,0:T(1,128)} %get-tuple-element.5) | copy-start | bytes 1540

commit v4 on v3

--- a/solution.py
+++ b/solution.py
@@ -169,7 +169,7 @@
 
         ways = (1, 3) if ring else (1, 3, 2)
         one, two, last = {}, {}, []
-        for d in (1, 3, 2):
+        for d in (2, 1, 3):
             for h in range(2):
                 one[h, d] = send(slot(h, 0, 0), first(h, d))
         for e in ways:
@@ -373,7 +373,7 @@
             )
 
         def send_all(h, q):
-            for p in (1, 3, 2):
+            for p in (2, 1, 3):
                 send_one(h, p, q)
 
         prepare(wrap(z + 2))

time: 124 us -> 124 us (level)
  no operation moved by 1% of the time
where the time goes in v4:
time: 124 us
  Pallas kernels  120 us (97%)
  other arithmetic  2.19 us (2%)
    pallas_call x1, Pallas kernels, body(): pl.pallas_call(kernel, out_shape=(jax.ShapeDtypeStruct((1, n), F32),) + (...  120 us

profile of v4, /device:TPU:0, one launch (start us, length us, event | category | flops | bytes accessed | tf_op | source)
XLA Modules:
  0.0 123.7 jit_solution(12208018482076405320)
XLA Ops:
  0.6 120.3 %patch_step.1 = (f32[1,128]{1,0:T(1,128)}, f32[128,1280]{1,0:T(8,128)}, f32[128,1280]{1,0:T(8,128)}) custom-call(bf16[128,1280]{1,0:T(8,128)(2,1)} %states.1, s32[1,128]{1,0:T(1,128)} %bitcast.8, s32[1,128]{1,0:T(1,128)} %bitcast.9, f32[1,128]{1,0:T(1,128)} %bitcast.10, bf16[1280,256]{1,0:T(8,128)(2,1)} %w_in.1, bf16[448,512]{1,0:T(8,128)(2,1)} %bitcast.6, ...), custom_call_target="tpu_custom_call" | custom-call | tf_op jit(solution)/shard_map/patch_step/pallas_call | solution.py:521
  121.0 0.0 copy-start
  121.0 2.2 %add.3 = f32[128,1280]{1,0:T(8,128)} add(f32[128,1280]{1,0:T(8,128)} %get-tuple-element.6, f32[128,1280]{1,0:T(8,128)} %get-tuple-element.7) | non-fusion elementwise | flops 163840 | bytes 1966080 | tf_op jit(solution)/shard_map/add | solution.py:535
  123.2 0.0 copy-done
  123.2 0.5 copy.14
Async XLA Ops:
  121.0 2.2 %copy-start = (f32[1,128]{1,0:T(1,128)S(1)}, f32[1,128]{1,0:T(1,128)}, u32[]{:S(2)}) copy-start(f32[1,128]{1,0:T(1,128)} %get-tuple-element.5) | copy-start | bytes 1540
